TPU v7x, 32 devices: a whole 2x2x4 slice. The times are simulated.
32 devices in a mesh: row: 2 (over core), col: 4 (over y, x), layer: 4 (over z).
Axes of the slice: x: 2, y: 2, z: 4, core: 2. Of those that a mesh axis runs over, the one named last changes fastest.
Arguments:
- blocks: bfloat16 [128, 24, 128, 128], P(('row', 'col'), 'layer'), may hold values from -2 to 2
- pattern: int32 [128, 24], replicated, may hold values from 0 to 127, as said below
- out_pattern: int32 [128, 24], replicated, may hold values from 0 to 127, as said below
Outputs:
- product: bfloat16 [128, 24, 128, 128], P(('row', 'col'), 'layer')
Inputs may be any that keep to these rules, and one draw needn't show every extreme that they name: `pattern`: block row i stores the block columns (i + d) mod 128 for 24 distinct offsets d from -12 to 12, always including 0, -12 and 12, in no particular order. `out_pattern`: the same law as pattern, drawn independently.
All inputs are finite; a program needn't handle non-finite values.
Results may differ from a plain program's by a relative error of at most 0.001.
Values may be sent and summed in bfloat16 or wider, within the bound.
A program may use at most 192 MiB of HBM per device.

v0:
```python
import jax
import jax.numpy as jnp
from jax import lax
from jax.sharding import PartitionSpec as P

REACH = 12


def with_halo(cells, sides, width):
    for axis, dim in sides:
        count = lax.axis_size(axis)
        head = lax.slice_in_dim(cells, 0, width, axis=dim)
        tail = lax.slice_in_dim(cells, cells.shape[dim] - width, cells.shape[dim], axis=dim)
        cells = jnp.concatenate(
            [
                lax.ppermute(tail, axis, [(i, (i + 1) % count) for i in range(count)]),
                cells,
                lax.ppermute(head, axis, [((i + 1) % count, i) for i in range(count)]),
            ],
            axis=dim,
        )
    return cells


def row_terms(left, right, right_cols, out_cols):
    match = right_cols[:, :, None] == out_cols[None, None, :]
    found = jnp.any(match, axis=1)
    picked = jnp.argmax(match.astype(jnp.int32), axis=1)
    chosen = jnp.take_along_axis(right, picked[:, :, None, None], axis=1)
    chosen = jnp.where(found[:, :, None, None], chosen, jnp.zeros((), right.dtype))
    return jnp.einsum("tab,tsbc->sac", left, chosen, preferred_element_type=jnp.float32)


def run_rows(left, left_cols, out_cols, outer, pattern, lowest):
    total_rows = pattern.shape[0]

    def one_row(item):
        piece, piece_cols, wanted = item
        where = (piece_cols - lowest) % total_rows
        right = jnp.take(outer, where, axis=0)
        right_cols = jnp.take(pattern, piece_cols, axis=0)
        return row_terms(piece, right, right_cols, wanted)

    return lax.map(one_row, (left, left_cols, out_cols))


def per_device(blocks, pattern, out_pattern):
    rows_dev = blocks.shape[0]
    slot_dev = blocks.shape[1]
    first = lax.axis_index(("row", "col")) * rows_dev
    layer_start = lax.axis_index("layer") * slot_dev
    own_cols = lax.dynamic_slice_in_dim(pattern, first, rows_dev, 0)
    own_out = lax.dynamic_slice_in_dim(out_pattern, first, rows_dev, 0)
    lowest = first - REACH
    whole = lax.all_gather(blocks, "layer", axis=1, tiled=True)
    outer = with_halo(whole, ((("row", "col"), 0),), REACH)
    mine_out = lax.dynamic_slice_in_dim(own_out, layer_start, slot_dev, 1)
    partial_value = run_rows(whole, own_cols, mine_out, outer, pattern, lowest)
    result = partial_value.astype(jnp.bfloat16)
    return result


def solution(mesh):
    in_specs = (P(("row", "col"), "layer", None, None), P(), P())
    out_specs = P(("row", "col"), "layer", None, None)
    return jax.shard_map(
        per_device, mesh=mesh, in_specs=in_specs, out_specs=out_specs, check_vma=False
    )
```

profile of v0, /device:TPU:0, one launch (start us, length us, event | category | flops | bytes accessed | tf_op | source)
XLA Modules:
  0.0 1751.4 jit_solution(12724038000201543942)
XLA Ops:
  7.3 222.6 %all-gather.2.cloned.1.call-done = bf16[16,24,128,128]{3,2,1,0:T(8,128)(2,1)} async-done(((bf16[16,6,128,128]{3,2,1,0:T(8,128)(2,1)}), bf16[16,24,128,128]{3,2,1,0:T(8,128)(2,1)}) %all-gather.2.cloned.1.call-update) | async-done | bytes 12582928 | tf_op jit(solution)/shard_map/all_gather | solution.py:55
  248.4 202.6 %collective-permute-done = bf16[12,24,128,128]{3,2,1,0:T(8,128)(2,1)} collective-permute-done((bf16[12,24,128,128]{3,2,1,0:T(8,128)(2,1)}, bf16[12,24,128,128]{3,2,1,0:T(8,128)(2,1)}, u32[]{:S(2)}, u32[]{:S(2)}) %collective-permute-start) | collective-permute-done | bytes 9437216 | tf_op jit(solution)/shard_map/ppermute | solution.py:16
  450.9 202.1 %collective-permute-done.1 = bf16[12,24,128,128]{3,2,1,0:T(8,128)(2,1)} collective-permute-done((bf16[12,24,128,128]{3,2,1,0:T(8,128)(2,1)}, bf16[12,24,128,128]{3,2,1,0:T(8,128)(2,1)}, u32[]{:S(2)}, u32[]{:S(2)}) %collective-permute-start.1) | collective-permute-done | bytes 9437216 | tf_op jit(solution)/shard_map/ppermute | solution.py:18
  653.1 21.8 %pad_maximum_fusion = bf16[40,24,128,128]{3,2,1,0:T(8,128)(2,1)} fusion(bf16[12,24,128,128]{3,2,1,0:T(8,128)(2,1)} %collective-permute-done.1, bf16[16,24,128,128]{3,2,1,0:T(8,128)(2,1)} %all-gather.2.cloned.1.call-done, bf16[12,24,128,128]{3,2,1,0:T(8,128)(2,1)} %collective-permute-done), kind=kLoop, calls=%fused_computation.48 | loop fusion | flops 31457280 | bytes 62914560 | tf_op jit(solution)/shard_map/concatenate | solution.py:14
  674.8 1066.9 %while.12 = (s32[]{:T(128)}, bf16[16,6,128,128]{2,3,1,0:T(8,128)(2,1)S(1)}, s32[16,24]{1,0:T(8,128)S(1)}, s32[128,24]{1,0:T(8,128)S(1)}, s32[16,6]{1,0:T(8,128)S...) while((s32[]{:T(128)}, ...), condition=%wide.region_3.4_spmd, body=%wide.region_0.3_spmd.sunk | while | flops 618178048 | bytes 100303056 | solution.py:44
  677.0 18.2 %gather_fusion = bf16[24,24,128,128]{3,2,1,0:T(8,128)(2,1)} fusion(bf16[40,24,128,128]{3,2,1,0:T(8,128)(2,1)} %get-tuple-element.244, s32[1024]{0:T(1024)S(1)} %get-tuple-element.216), kind=kCustom, calls=%fused_computation.1.clone.1 | custom fusion | bytes 37748832 | tf_op jit(solution)/shard_map/while/body/eval_jaxpr/jit(_take)/gather | solution.py:40
  695.2 17.0 broadcast_select_fusion.4
  712.2 18.5 %gather_fusion.2 = bf16[144,128,128]{2,1,0:T(8,128)(2,1)} fusion(bf16[24,24,128,128]{3,2,1,0:T(8,128)(2,1)} %broadcast_select_fusion.4, s32[144]{0:T(256)S(1)} %reshape.186), kind=kCustom, calls=%fused_computation.2.clone.1 | custom fusion | bytes 9438336 | tf_op jit(solution)/shard_map/while/body/eval_jaxpr/jit(take_along_axis)/gather | solution.py:29
  743.7 18.2 %gather_fusion = bf16[24,24,128,128]{3,2,1,0:T(8,128)(2,1)} fusion(bf16[40,24,128,128]{3,2,1,0:T(8,128)(2,1)} %get-tuple-element.244, s32[1024]{0:T(1024)S(1)} %get-tuple-element.216), kind=kCustom, calls=%fused_computation.1.clone.1 | custom fusion | bytes 37748832 | tf_op jit(solution)/shard_map/while/body/eval_jaxpr/jit(_take)/gather | solution.py:40
  761.9 17.0 broadcast_select_fusion.4
  778.9 18.5 %gather_fusion.2 = bf16[144,128,128]{2,1,0:T(8,128)(2,1)} fusion(bf16[24,24,128,128]{3,2,1,0:T(8,128)(2,1)} %broadcast_select_fusion.4, s32[144]{0:T(256)S(1)} %reshape.186), kind=kCustom, calls=%fused_computation.2.clone.1 | custom fusion | bytes 9438336 | tf_op jit(solution)/shard_map/while/body/eval_jaxpr/jit(take_along_axis)/gather | solution.py:29
  810.3 18.2 %gather_fusion = bf16[24,24,128,128]{3,2,1,0:T(8,128)(2,1)} fusion(bf16[40,24,128,128]{3,2,1,0:T(8,128)(2,1)} %get-tuple-element.244, s32[1024]{0:T(1024)S(1)} %get-tuple-element.216), kind=kCustom, calls=%fused_computation.1.clone.1 | custom fusion | bytes 37748832 | tf_op jit(solution)/shard_map/while/body/eval_jaxpr/jit(_take)/gather | solution.py:40
  828.6 17.0 broadcast_select_fusion.4
  845.6 18.5 %gather_fusion.2 = bf16[144,128,128]{2,1,0:T(8,128)(2,1)} fusion(bf16[24,24,128,128]{3,2,1,0:T(8,128)(2,1)} %broadcast_select_fusion.4, s32[144]{0:T(256)S(1)} %reshape.186), kind=kCustom, calls=%fused_computation.2.clone.1 | custom fusion | bytes 9438336 | tf_op jit(solution)/shard_map/while/body/eval_jaxpr/jit(take_along_axis)/gather | solution.py:29
  877.0 18.2 %gather_fusion = bf16[24,24,128,128]{3,2,1,0:T(8,128)(2,1)} fusion(bf16[40,24,128,128]{3,2,1,0:T(8,128)(2,1)} %get-tuple-element.244, s32[1024]{0:T(1024)S(1)} %get-tuple-element.216), kind=kCustom, calls=%fused_computation.1.clone.1 | custom fusion | bytes 37748832 | tf_op jit(solution)/shard_map/while/body/eval_jaxpr/jit(_take)/gather | solution.py:40
  895.2 17.0 broadcast_select_fusion.4
  912.3 18.5 %gather_fusion.2 = bf16[144,128,128]{2,1,0:T(8,128)(2,1)} fusion(bf16[24,24,128,128]{3,2,1,0:T(8,128)(2,1)} %broadcast_select_fusion.4, s32[144]{0:T(256)S(1)} %reshape.186), kind=kCustom, calls=%fused_computation.2.clone.1 | custom fusion | bytes 9438336 | tf_op jit(solution)/shard_map/while/body/eval_jaxpr/jit(take_along_axis)/gather | solution.py:29
  943.7 18.2 %gather_fusion = bf16[24,24,128,128]{3,2,1,0:T(8,128)(2,1)} fusion(bf16[40,24,128,128]{3,2,1,0:T(8,128)(2,1)} %get-tuple-element.244, s32[1024]{0:T(1024)S(1)} %get-tuple-element.216), kind=kCustom, calls=%fused_computation.1.clone.1 | custom fusion | bytes 37748832 | tf_op jit(solution)/shard_map/while/body/eval_jaxpr/jit(_take)/gather | solution.py:40
  961.9 17.0 broadcast_select_fusion.4
  979.0 18.5 %gather_fusion.2 = bf16[144,128,128]{2,1,0:T(8,128)(2,1)} fusion(bf16[24,24,128,128]{3,2,1,0:T(8,128)(2,1)} %broadcast_select_fusion.4, s32[144]{0:T(256)S(1)} %reshape.186), kind=kCustom, calls=%fused_computation.2.clone.1 | custom fusion | bytes 9438336 | tf_op jit(solution)/shard_map/while/body/eval_jaxpr/jit(take_along_axis)/gather | solution.py:29
  1010.4 18.2 %gather_fusion = bf16[24,24,128,128]{3,2,1,0:T(8,128)(2,1)} fusion(bf16[40,24,128,128]{3,2,1,0:T(8,128)(2,1)} %get-tuple-element.244, s32[1024]{0:T(1024)S(1)} %get-tuple-element.216), kind=kCustom, calls=%fused_computation.1.clone.1 | custom fusion | bytes 37748832 | tf_op jit(solution)/shard_map/while/body/eval_jaxpr/jit(_take)/gather | solution.py:40
  1045.6 18.5 %gather_fusion.2 = bf16[144,128,128]{2,1,0:T(8,128)(2,1)} fusion(bf16[24,24,128,128]{3,2,1,0:T(8,128)(2,1)} %broadcast_select_fusion.4, s32[144]{0:T(256)S(1)} %reshape.186), kind=kCustom, calls=%fused_computation.2.clone.1 | custom fusion | bytes 9438336 | tf_op jit(solution)/shard_map/while/body/eval_jaxpr/jit(take_along_axis)/gather | solution.py:29
  1077.1 18.2 %gather_fusion = bf16[24,24,128,128]{3,2,1,0:T(8,128)(2,1)} fusion(bf16[40,24,128,128]{3,2,1,0:T(8,128)(2,1)} %get-tuple-element.244, s32[1024]{0:T(1024)S(1)} %get-tuple-element.216), kind=kCustom, calls=%fused_computation.1.clone.1 | custom fusion | bytes 37748832 | tf_op jit(solution)/shard_map/while/body/eval_jaxpr/jit(_take)/gather | solution.py:40
  1112.3 18.5 %gather_fusion.2 = bf16[144,128,128]{2,1,0:T(8,128)(2,1)} fusion(bf16[24,24,128,128]{3,2,1,0:T(8,128)(2,1)} %broadcast_select_fusion.4, s32[144]{0:T(256)S(1)} %reshape.186), kind=kCustom, calls=%fused_computation.2.clone.1 | custom fusion | bytes 9438336 | tf_op jit(solution)/shard_map/while/body/eval_jaxpr/jit(take_along_axis)/gather | solution.py:29
  1143.7 18.2 %gather_fusion = bf16[24,24,128,128]{3,2,1,0:T(8,128)(2,1)} fusion(bf16[40,24,128,128]{3,2,1,0:T(8,128)(2,1)} %get-tuple-element.244, s32[1024]{0:T(1024)S(1)} %get-tuple-element.216), kind=kCustom, calls=%fused_computation.1.clone.1 | custom fusion | bytes 37748832 | tf_op jit(solution)/shard_map/while/body/eval_jaxpr/jit(_take)/gather | solution.py:40
  1179.0 18.5 %gather_fusion.2 = bf16[144,128,128]{2,1,0:T(8,128)(2,1)} fusion(bf16[24,24,128,128]{3,2,1,0:T(8,128)(2,1)} %broadcast_select_fusion.4, s32[144]{0:T(256)S(1)} %reshape.186), kind=kCustom, calls=%fused_computation.2.clone.1 | custom fusion | bytes 9438336 | tf_op jit(solution)/shard_map/while/body/eval_jaxpr/jit(take_along_axis)/gather | solution.py:29
  1210.4 18.2 %gather_fusion = bf16[24,24,128,128]{3,2,1,0:T(8,128)(2,1)} fusion(bf16[40,24,128,128]{3,2,1,0:T(8,128)(2,1)} %get-tuple-element.244, s32[1024]{0:T(1024)S(1)} %get-tuple-element.216), kind=kCustom, calls=%fused_computation.1.clone.1 | custom fusion | bytes 37748832 | tf_op jit(solution)/shard_map/while/body/eval_jaxpr/jit(_take)/gather | solution.py:40
  1228.7 17.0 broadcast_select_fusion.4
  1245.7 18.5 %gather_fusion.2 = bf16[144,128,128]{2,1,0:T(8,128)(2,1)} fusion(bf16[24,24,128,128]{3,2,1,0:T(8,128)(2,1)} %broadcast_select_fusion.4, s32[144]{0:T(256)S(1)} %reshape.186), kind=kCustom, calls=%fused_computation.2.clone.1 | custom fusion | bytes 9438336 | tf_op jit(solution)/shard_map/while/body/eval_jaxpr/jit(take_along_axis)/gather | solution.py:29
  1277.1 18.2 %gather_fusion = bf16[24,24,128,128]{3,2,1,0:T(8,128)(2,1)} fusion(bf16[40,24,128,128]{3,2,1,0:T(8,128)(2,1)} %get-tuple-element.244, s32[1024]{0:T(1024)S(1)} %get-tuple-element.216), kind=kCustom, calls=%fused_computation.1.clone.1 | custom fusion | bytes 37748832 | tf_op jit(solution)/shard_map/while/body/eval_jaxpr/jit(_take)/gather | solution.py:40
  1295.3 17.0 broadcast_select_fusion.4
  1312.4 18.5 %gather_fusion.2 = bf16[144,128,128]{2,1,0:T(8,128)(2,1)} fusion(bf16[24,24,128,128]{3,2,1,0:T(8,128)(2,1)} %broadcast_select_fusion.4, s32[144]{0:T(256)S(1)} %reshape.186), kind=kCustom, calls=%fused_computation.2.clone.1 | custom fusion | bytes 9438336 | tf_op jit(solution)/shard_map/while/body/eval_jaxpr/jit(take_along_axis)/gather | solution.py:29
  1343.8 18.2 %gather_fusion = bf16[24,24,128,128]{3,2,1,0:T(8,128)(2,1)} fusion(bf16[40,24,128,128]{3,2,1,0:T(8,128)(2,1)} %get-tuple-element.244, s32[1024]{0:T(1024)S(1)} %get-tuple-element.216), kind=kCustom, calls=%fused_computation.1.clone.1 | custom fusion | bytes 37748832 | tf_op jit(solution)/shard_map/while/body/eval_jaxpr/jit(_take)/gather | solution.py:40
  1362.0 17.0 broadcast_select_fusion.4
  1379.1 18.5 %gather_fusion.2 = bf16[144,128,128]{2,1,0:T(8,128)(2,1)} fusion(bf16[24,24,128,128]{3,2,1,0:T(8,128)(2,1)} %broadcast_select_fusion.4, s32[144]{0:T(256)S(1)} %reshape.186), kind=kCustom, calls=%fused_computation.2.clone.1 | custom fusion | bytes 9438336 | tf_op jit(solution)/shard_map/while/body/eval_jaxpr/jit(take_along_axis)/gather | solution.py:29
  1410.5 18.2 %gather_fusion = bf16[24,24,128,128]{3,2,1,0:T(8,128)(2,1)} fusion(bf16[40,24,128,128]{3,2,1,0:T(8,128)(2,1)} %get-tuple-element.244, s32[1024]{0:T(1024)S(1)} %get-tuple-element.216), kind=kCustom, calls=%fused_computation.1.clone.1 | custom fusion | bytes 37748832 | tf_op jit(solution)/shard_map/while/body/eval_jaxpr/jit(_take)/gather | solution.py:40
  1428.7 17.0 broadcast_select_fusion.4
  1445.7 18.5 %gather_fusion.2 = bf16[144,128,128]{2,1,0:T(8,128)(2,1)} fusion(bf16[24,24,128,128]{3,2,1,0:T(8,128)(2,1)} %broadcast_select_fusion.4, s32[144]{0:T(256)S(1)} %reshape.186), kind=kCustom, calls=%fused_computation.2.clone.1 | custom fusion | bytes 9438336 | tf_op jit(solution)/shard_map/while/body/eval_jaxpr/jit(take_along_axis)/gather | solution.py:29
  1477.2 18.2 %gather_fusion = bf16[24,24,128,128]{3,2,1,0:T(8,128)(2,1)} fusion(bf16[40,24,128,128]{3,2,1,0:T(8,128)(2,1)} %get-tuple-element.244, s32[1024]{0:T(1024)S(1)} %get-tuple-element.216), kind=kCustom, calls=%fused_computation.1.clone.1 | custom fusion | bytes 37748832 | tf_op jit(solution)/shard_map/while/body/eval_jaxpr/jit(_take)/gather | solution.py:40
  1495.4 17.0 broadcast_select_fusion.4
  1512.4 18.5 %gather_fusion.2 = bf16[144,128,128]{2,1,0:T(8,128)(2,1)} fusion(bf16[24,24,128,128]{3,2,1,0:T(8,128)(2,1)} %broadcast_select_fusion.4, s32[144]{0:T(256)S(1)} %reshape.186), kind=kCustom, calls=%fused_computation.2.clone.1 | custom fusion | bytes 9438336 | tf_op jit(solution)/shard_map/while/body/eval_jaxpr/jit(take_along_axis)/gather | solution.py:29
  1543.8 18.2 %gather_fusion = bf16[24,24,128,128]{3,2,1,0:T(8,128)(2,1)} fusion(bf16[40,24,128,128]{3,2,1,0:T(8,128)(2,1)} %get-tuple-element.244, s32[1024]{0:T(1024)S(1)} %get-tuple-element.216), kind=kCustom, calls=%fused_computation.1.clone.1 | custom fusion | bytes 37748832 | tf_op jit(solution)/shard_map/while/body/eval_jaxpr/jit(_take)/gather | solution.py:40
  1579.1 18.5 %gather_fusion.2 = bf16[144,128,128]{2,1,0:T(8,128)(2,1)} fusion(bf16[24,24,128,128]{3,2,1,0:T(8,128)(2,1)} %broadcast_select_fusion.4, s32[144]{0:T(256)S(1)} %reshape.186), kind=kCustom, calls=%fused_computation.2.clone.1 | custom fusion | bytes 9438336 | tf_op jit(solution)/shard_map/while/body/eval_jaxpr/jit(take_along_axis)/gather | solution.py:29
  1610.5 18.2 %gather_fusion = bf16[24,24,128,128]{3,2,1,0:T(8,128)(2,1)} fusion(bf16[40,24,128,128]{3,2,1,0:T(8,128)(2,1)} %get-tuple-element.244, s32[1024]{0:T(1024)S(1)} %get-tuple-element.216), kind=kCustom, calls=%fused_computation.1.clone.1 | custom fusion | bytes 37748832 | tf_op jit(solution)/shard_map/while/body/eval_jaxpr/jit(_take)/gather | solution.py:40
  1645.8 18.5 %gather_fusion.2 = bf16[144,128,128]{2,1,0:T(8,128)(2,1)} fusion(bf16[24,24,128,128]{3,2,1,0:T(8,128)(2,1)} %broadcast_select_fusion.4, s32[144]{0:T(256)S(1)} %reshape.186), kind=kCustom, calls=%fused_computation.2.clone.1 | custom fusion | bytes 9438336 | tf_op jit(solution)/shard_map/while/body/eval_jaxpr/jit(take_along_axis)/gather | solution.py:29
  1677.2 18.2 %gather_fusion = bf16[24,24,128,128]{3,2,1,0:T(8,128)(2,1)} fusion(bf16[40,24,128,128]{3,2,1,0:T(8,128)(2,1)} %get-tuple-element.244, s32[1024]{0:T(1024)S(1)} %get-tuple-element.216), kind=kCustom, calls=%fused_computation.1.clone.1 | custom fusion | bytes 37748832 | tf_op jit(solution)/shard_map/while/body/eval_jaxpr/jit(_take)/gather | solution.py:40
  1695.4 17.0 broadcast_select_fusion.4
  1712.5 18.5 %gather_fusion.2 = bf16[144,128,128]{2,1,0:T(8,128)(2,1)} fusion(bf16[24,24,128,128]{3,2,1,0:T(8,128)(2,1)} %broadcast_select_fusion.4, s32[144]{0:T(256)S(1)} %reshape.186), kind=kCustom, calls=%fused_computation.2.clone.1 | custom fusion | bytes 9438336 | tf_op jit(solution)/shard_map/while/body/eval_jaxpr/jit(take_along_axis)/gather | solution.py:29
  (258 shorter events, 312.6 us)
Async XLA Ops:
  6.5 223.3 %all-gather.2.cloned.1.call-start = ((), (), s32[]{:S(2)}) async-start(), calls=%async_computation | async-start | bytes 15728640 | tf_op jit(solution)/shard_map/all_gather | solution.py:55
  7.3 241.0 %copy-start = (s32[128,24]{0,1:T(8,128)S(1)}, s32[128,24]{0,1:T(8,128)}, u32[]{:S(2)}) copy-start(s32[128,24]{0,1:T(8,128)} %param.6) | copy-start | bytes 36868
  244.7 206.2 %collective-permute-start = (bf16[12,24,128,128]{3,2,1,0:T(8,128)(2,1)}, bf16[12,24,128,128]{3,2,1,0:T(8,128)(2,1)}, u32[]{:S(2)}, u32[]{:S(2)}) collective-permute-start(bf16[12,24,128,128]{3,2,1,0:T(8,128)(2,1)} %get-tuple-element.155), channel_id=1, source_target_pairs={{0,4},{4,8},{8,12},{12,16},{16,20},{20,24},{24,28},{28,0},{1,5},{5... | collective-permute-start | bytes 28311560 | tf_op jit(solution)/shard_map/ppermute | solution.py:16
  246.2 406.9 %collective-permute-start.1 = (bf16[12,24,128,128]{3,2,1,0:T(8,128)(2,1)}, bf16[12,24,128,128]{3,2,1,0:T(8,128)(2,1)}, u32[]{:S(2)}, u32[]{:S(2)}) collective-permute-start(bf16[12,24,128,128]{3,2,1,0:T(8,128)(2,1)} %get-tuple-element.156), channel_id=1, source_target_pairs={{4,0},{8,4},{12,8},{16,12},{20,16},{24,20},{28,24},{0,28},{5,1},{9... | collective-permute-start | bytes 28311560 | tf_op jit(solution)/shard_map/ppermute | solution.py:18
Sparse Core Ops, SparseCore 0:
  8.9 220.8 all-gather.1
where the time goes:
time: 1760 us; the launch traced here: 1750 us
  local copies, waits for them, and re-layouts  725 us (41%)
  waiting for transfers between devices  628 us (36%)
  other arithmetic  315 us (18%)
  matrix products  65.3 us (4%)
    gather x64, local copies, waits for them, and re-layouts, row_terms(): chosen = jnp.take_along_axis(right, picked[:, :, None, None], axis=1)  406 us
    gather x16, local copies, waits for them, and re-layouts, one_row(): right = jnp.take(outer, where, axis=0)  292 us
    select_n x16, other arithmetic, one_row(): right = jnp.take(outer, where, axis=0)  273 us
    all_gather x1, waiting for transfers between devices, per_device(): whole = lax.all_gather(blocks, 'layer', axis=1, tiled=True)  223 us
    ppermute x1, waiting for transfers between devices, with_halo(): lax.ppermute(tail, axis, [(i, (i + 1) % count) for i in range(count)])  203 us
    ppermute x1, waiting for transfers between devices, with_halo(): lax.ppermute(head, axis, [((i + 1) % count, i) for i in range(count)])  202 us
    dot_general x16, matrix products, row_terms(): jnp.einsum('tab,tsbc->sac', left, chosen, preferred_element_type=jnp.floa...  65.3 us
  transfers between devices with their start and end apart: 3, of which 3 were waited for; matrix products, arithmetic and copies ran while one was open for 0% of the time, Pallas kernels for 0%

commit v1 on v0

v1 whole, which is shorter than its diff:
```python
import functools

import jax
import jax.numpy as jnp
from jax import lax
from jax.experimental import pallas as pl
from jax.experimental.pallas import tpu as pltpu
from jax.sharding import PartitionSpec as P

REACH = 12
DIRECT = 6
MESH = pl.DeviceIdType.MESH


def gather_kernel(shape, blocks, full, local_sem, near_send, near_recv, far_send, far_recv, z_send, z_recv):
    rows_n, cols_n, layers = shape
    rows, slots = blocks.shape[:2]
    groups = rows_n * cols_n
    layer = lax.axis_index("layer")
    group = lax.axis_index("row") * cols_n + lax.axis_index("col")

    def at_group(g):
        return (lax.div(g, cols_n), lax.rem(g, cols_n), layer)

    right = at_group(lax.rem(group + 1, groups))
    left = at_group(lax.rem(group + groups - 1, groups))
    up = (lax.axis_index("row"), lax.axis_index("col"), lax.min(layer + 1, layers - 1))
    down = (lax.axis_index("row"), lax.axis_index("col"), lax.max(layer - 1, 0))
    has_up = layer < layers - 1
    has_down = layer > 0

    def own(first, count):
        return blocks.at[pl.ds(first, count)]

    def part(first, count, g):
        return full.at[pl.ds(first, count), pl.ds(g * slots, slots)]

    far = REACH - DIRECT
    half = rows // 2
    pieces = (
        (REACH, half),
        (REACH + half, rows - half),
        (REACH - DIRECT, DIRECT),
        (REACH + rows, DIRECT),
    )

    barrier = pltpu.get_barrier_semaphore()
    for other in (left, right):
        pl.semaphore_signal(barrier, inc=1, device_id=other, device_id_type=MESH)

    @pl.when(has_up)
    def _():
        pl.semaphore_signal(barrier, inc=1, device_id=up, device_id_type=MESH)

    @pl.when(has_down)
    def _():
        pl.semaphore_signal(barrier, inc=1, device_id=down, device_id_type=MESH)

    pl.semaphore_wait(barrier, 2 + has_up.astype(jnp.int32) + has_down.astype(jnp.int32))

    def remote(src, dst, send, recv, target):
        return pltpu.make_async_remote_copy(
            src_ref=src, dst_ref=dst, send_sem=send, recv_sem=recv, device_id=target, device_id_type=MESH
        )

    keep = pltpu.make_async_copy(blocks, part(REACH, rows, layer), local_sem)
    keep.start()

    near_right = remote(own(rows - DIRECT, DIRECT), part(REACH - DIRECT, DIRECT, layer), near_send.at[0], near_recv.at[0], right)
    near_left = remote(own(0, DIRECT), part(REACH + rows, DIRECT, layer), near_send.at[1], near_recv.at[1], left)
    near_right.start()
    near_left.start()

    def along(p, g, direction, src=None):
        first, count = pieces[p]
        return remote(
            part(first, count, g) if src is None else src,
            part(first, count, g),
            z_send.at[p, direction, g],
            z_recv.at[p, g],
            up if direction == 0 else down,
        )

    def start_along(p, g, direction, src=None):
        @pl.when(has_up if direction == 0 else has_down)
        def _():
            along(p, g, direction, src).start()

    for p in (0, 1):
        src = own(pieces[p][0] - REACH, pieces[p][1])
        start_along(p, layer, 0, src)
        start_along(p, layer, 1, src)

    def far_copies(g, from_blocks=False):
        def of(first):
            return own(first, far) if from_blocks else part(REACH + first, far, g)

        to_right = remote(of(rows - REACH), part(0, far, g), far_send.at[0, g], far_recv.at[0, g], right)
        to_left = remote(of(DIRECT), part(REACH + rows + DIRECT, far, g), far_send.at[1, g], far_recv.at[1, g], left)
        return to_right, to_left

    for copy in far_copies(layer, True):
        copy.start()

    def forward(p, hop):
        @pl.when(layer >= hop)
        def _():
            g = layer - hop
            along(p, g, 0).wait_recv()
            start_along(p, g, 0)

        @pl.when(layer + hop < layers)
        def _():
            g = layer + hop
            along(p, g, 1).wait_recv()
            start_along(p, g, 1)

    def start_far(hop):
        @pl.when(layer >= hop)
        def _():
            for copy in far_copies(layer - hop):
                copy.start()

        @pl.when(layer + hop < layers)
        def _():
            for copy in far_copies(layer + hop):
                copy.start()

    for hop in range(1, layers):
        forward(0, hop)
        forward(1, hop)
        start_far(hop)
        if hop == 1:
            near_right.wait_recv()
            start_along(2, layer, 0)
            start_along(2, layer, 1)
            near_left.wait_recv()
            start_along(3, layer, 0)
            start_along(3, layer, 1)
        else:
            forward(2, hop - 1)
            forward(3, hop - 1)
    if layers == 1:
        near_right.wait_recv()
        near_left.wait_recv()
    else:
        forward(2, layers - 1)
        forward(3, layers - 1)

    for g in range(layers):
        for copy in far_copies(g):
            copy.wait()
    near_right.wait_send()
    near_left.wait_send()
    for p in range(4):
        for g in range(layers):
            @pl.when(has_up & (layer >= g))
            def _():
                along(p, g, 0).wait_send()

            @pl.when(has_down & (layer <= g))
            def _():
                along(p, g, 1).wait_send()

    keep.wait()


def gather_rows(blocks, shape):
    rows, slots = blocks.shape[:2]
    layers = shape[2]
    return pl.pallas_call(
        functools.partial(gather_kernel, shape),
        out_shape=jax.ShapeDtypeStruct((rows + 2 * REACH, slots * layers) + blocks.shape[2:], blocks.dtype),
        in_specs=[pl.BlockSpec(memory_space=pl.ANY)],
        out_specs=pl.BlockSpec(memory_space=pl.ANY),
        scratch_shapes=[
            pltpu.SemaphoreType.DMA,
            pltpu.SemaphoreType.DMA((2,)),
            pltpu.SemaphoreType.DMA((2,)),
            pltpu.SemaphoreType.DMA((2, layers)),
            pltpu.SemaphoreType.DMA((2, layers)),
            pltpu.SemaphoreType.DMA((4, 2, layers)),
            pltpu.SemaphoreType.DMA((4, layers)),
        ],
        compiler_params=pltpu.CompilerParams(collective_id=0, has_side_effects=True),
    )(blocks)


def multiply_kernel(picked, full, out, held, sems):
    row = pl.program_id(0)
    outer, slots = full.shape[:2]
    wanted = out.shape[1]

    def fetch(r):
        return pltpu.make_async_copy(full.at[r], held.at[pl.ds(r * slots, slots)], sems.at[r])

    @pl.when(row == 0)
    def _():
        @pl.loop(0, outer)
        def _(r):
            fetch(r).start()

        held[outer * slots] = jnp.zeros(held.shape[1:], held.dtype)

        @pl.loop(0, 2 * REACH)
        def _(r):
            fetch(r).wait()

    fetch(row + 2 * REACH).wait()

    mine = (row + REACH) * slots
    lhs = jnp.concatenate([held[mine + t] for t in range(slots)], axis=1)
    for s in range(0, wanted, 2):
        pair = range(s, min(s + 2, wanted))
        rhs = jnp.concatenate(
            [
                jnp.concatenate([held[picked[row, k * slots + t]] for k in pair], axis=1)
                for t in range(slots)
            ],
            axis=0,
        )
        sums = jnp.dot(lhs, rhs, preferred_element_type=jnp.float32).astype(out.dtype)
        for n, k in enumerate(pair):
            out[0, k] = sums[:, n * out.shape[3] : (n + 1) * out.shape[3]]


def multiply(full, picked, rows, wanted):
    outer, slots, size = full.shape[:3]
    return pl.pallas_call(
        multiply_kernel,
        out_shape=jax.ShapeDtypeStruct((rows, wanted, size, size), full.dtype),
        grid_spec=pltpu.PrefetchScalarGridSpec(
            num_scalar_prefetch=1,
            grid=(rows,),
            in_specs=[pl.BlockSpec(memory_space=pl.ANY)],
            out_specs=pl.BlockSpec((1, wanted, size, size), lambda i, picked: (i, 0, 0, 0)),
            scratch_shapes=[
                pltpu.VMEM((outer * slots + 1, size, size), full.dtype),
                pltpu.SemaphoreType.DMA((outer,)),
            ],
        ),
        compiler_params=pltpu.CompilerParams(
            dimension_semantics=("arbitrary",), vmem_limit_bytes=48 * 2**20
        ),
    )(picked, full)


def per_device(shape, blocks, pattern, out_pattern):
    rows, wanted = blocks.shape[:2]
    total, slots = pattern.shape
    outer = rows + 2 * REACH
    first = lax.axis_index(("row", "col")) * rows
    full = gather_rows(blocks, shape)
    own_cols = lax.dynamic_slice_in_dim(pattern, first, rows, 0)
    own_out = lax.dynamic_slice(out_pattern, (first, lax.axis_index("layer") * wanted), (rows, wanted))
    where = (own_cols - (first - REACH)) % total
    right_cols = jnp.take(pattern, own_cols, axis=0)
    match = right_cols[:, None, :, :] == own_out[:, :, None, None]
    slot = jnp.max(jnp.where(match, jnp.arange(1, slots + 1, dtype=jnp.int32), 0), axis=-1)
    picked = jnp.where(slot > 0, where[:, None, :] * slots + slot - 1, outer * slots)
    return multiply(full, picked.reshape(rows, wanted * slots), rows, wanted)


def solution(mesh):
    shape = tuple(mesh.shape[axis] for axis in ("row", "col", "layer"))
    spec = P(("row", "col"), "layer", None, None)
    return jax.shard_map(
        functools.partial(per_device, shape),
        mesh=mesh,
        in_specs=(spec, P(), P()),
        out_specs=spec,
        check_vma=False,
    )
```

time: 1760 us -> 388 us (0.22)
  local copies, waits for them, and re-layouts: 725 us -> 2.94 us
  waiting for transfers between devices: 628 us -> 0 us
  Pallas kernels: 0 us -> 383 us
  other arithmetic: 315 us -> 1.99 us
  matrix products: 65.3 us -> 0 us
    gather x96 -> x1, local copies, waits for them, and re-layouts: 707 us -> 1.12 us  [per_device(): right_cols = jnp.take(pattern, own_cols, axis=0)]
    ppermute x2 -> x0, waiting for transfers between devices: 405 us -> none  [the longest x1 203 us: with_halo(): lax.ppermute(tail, axis, [(i, (i + 1) % count) for i in range(count)])]
    pallas_call x0 -> x2, Pallas kernels: none -> 383 us  [the longest x1 361 us: gather_rows(): pl.pallas_call(functools.partial(gather_kernel, shape), out_shape=jax.Sha...]
    select_n x48 -> x2, other arithmetic: 274 us -> 0.13 us  [the longest x1 0.12 us: per_device(): right_cols = jnp.take(pattern, own_cols, axis=0)]
    all_gather x1 -> x0, waiting for transfers between devices: 223 us -> none  [per_device(): whole = lax.all_gather(blocks, 'layer', axis=1, tiled=True)]
    dot_general x16 -> x0, matrix products: 65.3 us -> none  [row_terms(): jnp.einsum('tab,tsbc->sac', left, chosen, preferred_element_type=jnp.floa...]
    concatenate x1 -> x0, other arithmetic: 21.8 us -> none  [with_halo(): jnp.concatenate([lax.ppermute(tail, axis, [(i, (i + 1) % count) for i in...]
  transfers between devices with their start and end apart: 3 -> 0, of which waited for: 3 -> 0; matrix products, arithmetic and copies ran while one was open for 0% -> 0% of each run, Pallas kernels for 0% -> 0%
where the time goes in v1:
time: 388 us
  Pallas kernels  383 us (99%)
    pallas_call x1, Pallas kernels, gather_rows(): pl.pallas_call(functools.partial(gather_kernel, shape), out_shape=jax.Sha...  361 us
    pallas_call x1, Pallas kernels, multiply(): pl.pallas_call(multiply_kernel, out_shape=jax.ShapeDtypeStruct((rows, wan...  21.4 us

profile of v1, /device:TPU:0, one launch (start us, length us, event | category | flops | bytes accessed | tf_op | source)
XLA Modules:
  0.0 387.8 jit_solution(9617364028323046806)
XLA Ops:
  0.0 0.8 dynamic_slice.7
  0.8 0.1 copy.20
  0.9 0.8 copy.18
  1.7 0.1 reshape.23
  1.8 1.1 gather_fusion
  2.9 0.1 broadcast_select_fusion
  3.1 1.8 select_reduce_fusion
  4.9 0.1 select_n.46.picked
  5.0 361.4 %shard_map.37.full = bf16[40,24,128,128]{3,2,1,0:T(8,128)(2,1)} custom-call(bf16[16,6,128,128]{3,2,1,0:T(8,128)(2,1)} %blocks.1), custom_call_target="tpu_custom_call" | custom-call | tf_op jit(solution)/shard_map/pallas_call | solution.py:171
  366.4 21.4 %shard_map.38 = bf16[16,6,128,128]{3,2,1,0:T(8,128)(2,1)} custom-call(s32[16,144]{1,0:T(8,128)S(1)} %select_n.46.picked, bf16[40,24,128,128]{3,2,1,0:T(8,128)(2,1)} %shard_map.37.full), custom_call_target="tpu_custom_call" | custom-call | tf_op jit(solution)/shard_map/pallas_call | solution.py:229
  (5 shorter events, 0.1 us)

commit v2 on v1

--- a/solution.py
+++ b/solution.py
@@ -8,7 +8,7 @@
 from jax.sharding import PartitionSpec as P
 
 REACH = 12
-DIRECT = 6
+DIRECT = 4
 MESH = pl.DeviceIdType.MESH
 
 

time: 388 us -> 338 us (0.87)
  Pallas kernels: 383 us -> 333 us
    pallas_call x1, Pallas kernels: 361 us -> 312 us  [gather_rows(): pl.pallas_call(functools.partial(gather_kernel, shape), out_shape=jax.Sha...]
where the time goes in v2:
time: 338 us
  Pallas kernels  333 us (99%)
    pallas_call x1, Pallas kernels, gather_rows(): pl.pallas_call(functools.partial(gather_kernel, shape), out_shape=jax.Sha...  312 us
    pallas_call x1, Pallas kernels, multiply(): pl.pallas_call(multiply_kernel, out_shape=jax.ShapeDtypeStruct((rows, wan...  21.4 us

profile of v2, /device:TPU:0, one launch (start us, length us, event | category | flops | bytes accessed | tf_op | source)
XLA Modules:
  0.0 338.0 jit_solution(17035593103669525588)
XLA Ops:
  0.0 0.8 dynamic_slice.7
  0.8 0.1 copy.20
  0.9 0.8 copy.18
  1.7 0.1 reshape.23
  1.8 1.1 gather_fusion
  2.9 0.1 broadcast_select_fusion
  3.1 1.8 select_reduce_fusion
  4.9 0.1 select_n.46.picked
  5.0 311.6 %shard_map.37.full = bf16[40,24,128,128]{3,2,1,0:T(8,128)(2,1)} custom-call(bf16[16,6,128,128]{3,2,1,0:T(8,128)(2,1)} %blocks.1), custom_call_target="tpu_custom_call" | custom-call | tf_op jit(solution)/shard_map/pallas_call | solution.py:171
  316.6 21.4 %shard_map.38 = bf16[16,6,128,128]{3,2,1,0:T(8,128)(2,1)} custom-call(s32[16,144]{1,0:T(8,128)S(1)} %select_n.46.picked, bf16[40,24,128,128]{3,2,1,0:T(8,128)(2,1)} %shard_map.37.full), custom_call_target="tpu_custom_call" | custom-call | tf_op jit(solution)/shard_map/pallas_call | solution.py:229
  (5 shorter events, 0.1 us)

commit v3 on v2

v3 whole, which is shorter than its diff:
```python
import functools

import jax
import jax.numpy as jnp
from jax import lax
from jax.experimental import pallas as pl
from jax.experimental.pallas import tpu as pltpu
from jax.sharding import PartitionSpec as P

REACH = 12
DIRECT = 1
PIECES = 8
MESH = pl.DeviceIdType.MESH


def gather_kernel(shape, blocks, full, local_sem, near_send, near_recv, far_send, far_recv, on_send, on_recv, z_send, z_recv):
    rows_n, cols_n, layers = shape
    rows, slots = blocks.shape[:2]
    groups = rows_n * cols_n
    row, col, layer = (lax.axis_index(axis) for axis in ("row", "col", "layer"))
    group = row * cols_n + col
    odd = lax.rem(group, 2)

    def at_group(g):
        g = lax.rem(g + groups, groups)
        return (lax.div(g, cols_n), lax.rem(g, cols_n), layer)

    right, left = at_group(group + 1), at_group(group - 1)
    partner = at_group(group + 1 - 2 * odd)
    beyond = at_group(group + 2 - 4 * odd)
    behind = at_group(group - 2 + 4 * odd)
    up = (row, col, lax.min(layer + 1, layers - 1))
    down = (row, col, lax.max(layer - 1, 0))
    has_up = layer < layers - 1
    has_down = layer > 0

    step = rows // PIECES
    pieces = tuple((rows + k * step, step) for k in range(PIECES)) + (
        (rows - DIRECT, DIRECT),
        (2 * rows, DIRECT),
    )
    before, after = (DIRECT, REACH), (rows - REACH, rows - DIRECT)

    def cut(k, low, high):
        first, last = max(k * step, low), min((k + 1) * step, high)
        return first, max(last - first, 0)

    def own(first, count):
        return blocks.at[pl.ds(first, count)]

    def part(first, count, g):
        return full.at[pl.ds(first, count), pl.ds(g * slots, slots)]

    barrier = pltpu.get_barrier_semaphore()
    for other in (left, right, beyond, behind):
        pl.semaphore_signal(barrier, inc=1, device_id=other, device_id_type=MESH)

    @pl.when(has_up)
    def _():
        pl.semaphore_signal(barrier, inc=1, device_id=up, device_id_type=MESH)

    @pl.when(has_down)
    def _():
        pl.semaphore_signal(barrier, inc=1, device_id=down, device_id_type=MESH)

    pl.semaphore_wait(barrier, 4 + has_up.astype(jnp.int32) + has_down.astype(jnp.int32))

    def remote(src, dst, send, recv, target):
        return pltpu.make_async_remote_copy(
            src_ref=src, dst_ref=dst, send_sem=send, recv_sem=recv, device_id=target, device_id_type=MESH
        )

    keep = pltpu.make_async_copy(blocks, part(rows, rows, layer), local_sem)
    keep.start()

    near_right = remote(own(rows - DIRECT, DIRECT), part(rows - DIRECT, DIRECT, layer), near_send.at[0], near_recv.at[0], right)
    near_left = remote(own(0, DIRECT), part(2 * rows, DIRECT, layer), near_send.at[1], near_recv.at[1], left)

    def along(p, g, direction, src=None):
        first, count = pieces[p]
        return remote(
            part(first, count, g) if src is None else src,
            part(first, count, g),
            z_send.at[p, direction, g],
            z_recv.at[p, g],
            up if direction == 0 else down,
        )

    def start_along(p, g, direction, src=None):
        @pl.when(has_up if direction == 0 else has_down)
        def _():
            along(p, g, direction, src).start()

    for k in range(PIECES):
        src = own(k * step, step)
        start_along(k, layer, 0, src)
        start_along(k, layer, 1, src)

    def far(k, g, from_blocks=False):
        first, count = cut(k, DIRECT, rows - DIRECT)
        src = own(first, count) if from_blocks else part(rows + first, count, g)
        return remote(src, part(odd * 2 * rows + first, count, g), far_send.at[k, g], far_recv.at[k, g], partner)

    def on(k, g, parity):
        first, count = cut(k, *(before if parity else after))
        if not count:
            return None
        return remote(
            part((0 if parity else 2 * rows) + first, count, g),
            part((2 * rows if parity else 0) + first, count, g),
            on_send.at[k, g],
            on_recv.at[k, g],
            beyond,
        )

    def pass_on(k, g):
        far(k, g).wait_recv()
        for parity in (0, 1):
            copy = on(k, g, parity)
            if copy is not None:
                pl.when(odd == parity)(copy.start)

    for k in range(PIECES):
        far(k, layer, True).start()
    near_right.start()
    near_left.start()

    def at_hop(hop, act):
        @pl.when(layer >= hop)
        def _():
            act(layer - hop, 0)

        @pl.when(layer + hop < layers)
        def _():
            act(layer + hop, 1)

    def forward(p, hop):
        def act(g, direction):
            along(p, g, direction).wait_recv()
            start_along(p, g, direction)
            if p < PIECES:
                far(p, g).start()

        at_hop(hop, act)

    edges = (PIECES, PIECES + 1)
    for hop in range(1, layers):
        for k in range(PIECES):
            forward(k, hop)
            if k == PIECES - 1 and hop > 1:
                for p in edges:
                    forward(p, hop - 1)
            if hop == 1:
                pass_on(k, layer)
            else:
                at_hop(hop - 1, lambda g, direction: pass_on(k, g))
        if hop == 1:
            near_right.wait_recv()
            near_left.wait_recv()
            for p in edges:
                start_along(p, layer, 0)
                start_along(p, layer, 1)
    for k in range(PIECES):
        at_hop(layers - 1, lambda g, direction: pass_on(k, g))
    for p in edges:
        forward(p, layers - 1)

    for g in range(layers):
        for k in range(PIECES):
            far(k, g).wait_send()
            for parity in (0, 1):
                copy = on(k, g, parity)
                if copy is not None:
                    pl.when(odd == parity)(copy.wait)
    near_right.wait_send()
    near_left.wait_send()
    for p in range(PIECES + 2):
        for g in range(layers):
            @pl.when(has_up & (layer >= g))
            def _():
                along(p, g, 0).wait_send()

            @pl.when(has_down & (layer <= g))
            def _():
                along(p, g, 1).wait_send()

    keep.wait()


def gather_rows(blocks, shape):
    rows, slots = blocks.shape[:2]
    layers = shape[2]
    return pl.pallas_call(
        functools.partial(gather_kernel, shape),
        out_shape=jax.ShapeDtypeStruct((3 * rows, slots * layers) + blocks.shape[2:], blocks.dtype),
        in_specs=[pl.BlockSpec(memory_space=pl.ANY)],
        out_specs=pl.BlockSpec(memory_space=pl.ANY),
        scratch_shapes=[
            pltpu.SemaphoreType.DMA,
            pltpu.SemaphoreType.DMA((2,)),
            pltpu.SemaphoreType.DMA((2,)),
            pltpu.SemaphoreType.DMA((PIECES, layers)),
            pltpu.SemaphoreType.DMA((PIECES, layers)),
            pltpu.SemaphoreType.DMA((PIECES, layers)),
            pltpu.SemaphoreType.DMA((PIECES, layers)),
            pltpu.SemaphoreType.DMA((PIECES + 2, 2, layers)),
            pltpu.SemaphoreType.DMA((PIECES + 2, layers)),
        ],
        compiler_params=pltpu.CompilerParams(collective_id=0, has_side_effects=True),
    )(blocks)


def multiply_kernel(picked, full, out, held, sems):
    row = pl.program_id(0)
    spare = full.shape[0] // 3 - REACH
    outer, slots = full.shape[0] - 2 * spare, full.shape[1]
    wanted = out.shape[1]

    def fetch(r):
        return pltpu.make_async_copy(full.at[spare + r], held.at[pl.ds(r * slots, slots)], sems.at[r])

    @pl.when(row == 0)
    def _():
        @pl.loop(0, outer)
        def _(r):
            fetch(r).start()

        held[outer * slots] = jnp.zeros(held.shape[1:], held.dtype)

        @pl.loop(0, 2 * REACH)
        def _(r):
            fetch(r).wait()

    fetch(row + 2 * REACH).wait()

    mine = (row + REACH) * slots
    lhs = jnp.concatenate([held[mine + t] for t in range(slots)], axis=1)
    for s in range(0, wanted, 2):
        pair = range(s, min(s + 2, wanted))
        rhs = jnp.concatenate(
            [
                jnp.concatenate([held[picked[row, k * slots + t]] for k in pair], axis=1)
                for t in range(slots)
            ],
            axis=0,
        )
        sums = jnp.dot(lhs, rhs, preferred_element_type=jnp.float32).astype(out.dtype)
        for n, k in enumerate(pair):
            out[0, k] = sums[:, n * out.shape[3] : (n + 1) * out.shape[3]]


def multiply(full, picked, rows, wanted):
    slots, size = full.shape[1:3]
    outer = rows + 2 * REACH
    return pl.pallas_call(
        multiply_kernel,
        out_shape=jax.ShapeDtypeStruct((rows, wanted, size, size), full.dtype),
        grid_spec=pltpu.PrefetchScalarGridSpec(
            num_scalar_prefetch=1,
            grid=(rows,),
            in_specs=[pl.BlockSpec(memory_space=pl.ANY)],
            out_specs=pl.BlockSpec((1, wanted, size, size), lambda i, picked: (i, 0, 0, 0)),
            scratch_shapes=[
                pltpu.VMEM((outer * slots + 1, size, size), full.dtype),
                pltpu.SemaphoreType.DMA((outer,)),
            ],
        ),
        compiler_params=pltpu.CompilerParams(
            dimension_semantics=("arbitrary",), vmem_limit_bytes=48 * 2**20
        ),
    )(picked, full)


def per_device(shape, blocks, pattern, out_pattern):
    rows, wanted = blocks.shape[:2]
    total, slots = pattern.shape
    outer = rows + 2 * REACH
    first = lax.axis_index(("row", "col")) * rows
    full = gather_rows(blocks, shape)
    own_cols = lax.dynamic_slice_in_dim(pattern, first, rows, 0)
    own_out = lax.dynamic_slice(out_pattern, (first, lax.axis_index("layer") * wanted), (rows, wanted))
    where = (own_cols - (first - REACH)) % total
    right_cols = jnp.take(pattern, own_cols, axis=0)
    match = right_cols[:, None, :, :] == own_out[:, :, None, None]
    slot = jnp.max(jnp.where(match, jnp.arange(1, slots + 1, dtype=jnp.int32), 0), axis=-1)
    picked = jnp.where(slot > 0, where[:, None, :] * slots + slot - 1, outer * slots)
    return multiply(full, picked.reshape(rows, wanted * slots), rows, wanted)


def solution(mesh):
    shape = tuple(mesh.shape[axis] for axis in ("row", "col", "layer"))
    spec = P(("row", "col"), "layer", None, None)
    return jax.shard_map(
        functools.partial(per_device, shape),
        mesh=mesh,
        in_specs=(spec, P(), P()),
        out_specs=spec,
        check_vma=False,
    )
```

time: 338 us -> 306 us (0.905)
  Pallas kernels: 333 us -> 301 us
    pallas_call x1, Pallas kernels: 312 us -> 280 us  [gather_rows(): pl.pallas_call(functools.partial(gather_kernel, shape), out_shape=jax.Sha...]
where the time goes in v3:
time: 306 us
  Pallas kernels  301 us (98%)
    pallas_call x1, Pallas kernels, gather_rows(): pl.pallas_call(functools.partial(gather_kernel, shape), out_shape=jax.Sha...  280 us
    pallas_call x1, Pallas kernels, multiply(): pl.pallas_call(multiply_kernel, out_shape=jax.ShapeDtypeStruct((rows, wan...  21.4 us

profile of v3, /device:TPU:0, one launch (start us, length us, event | category | flops | bytes accessed | tf_op | source)
XLA Modules:
  0.0 306.0 jit_solution(10087507888320239861)
XLA Ops:
  0.0 0.8 dynamic_slice.7
  0.8 0.1 copy.20
  0.9 0.8 copy.18
  1.7 0.1 reshape.23
  1.8 1.1 gather_fusion
  2.9 0.1 broadcast_select_fusion
  3.1 1.8 select_reduce_fusion
  4.9 0.1 select_n.46.picked
  5.0 279.6 %shard_map.37.full = bf16[48,24,128,128]{3,2,1,0:T(8,128)(2,1)} custom-call(bf16[16,6,128,128]{3,2,1,0:T(8,128)(2,1)} %blocks.1), custom_call_target="tpu_custom_call" | custom-call | tf_op jit(solution)/shard_map/pallas_call | solution.py:193
  284.6 21.4 %shard_map.38 = bf16[16,6,128,128]{3,2,1,0:T(8,128)(2,1)} custom-call(s32[16,144]{1,0:T(8,128)S(1)} %select_n.46.picked, bf16[48,24,128,128]{3,2,1,0:T(8,128)(2,1)} %shard_map.37.full), custom_call_target="tpu_custom_call" | custom-call | tf_op jit(solution)/shard_map/pallas_call | solution.py:255
  (5 shorter events, 0.1 us)
